TPU v7x, 32 devices: a whole 2x2x4 slice. The times are simulated.
32 devices in a mesh: band: 4 (over y, x), grid: 8 (over z, core).
Axes of the slice: x: 2, y: 2, z: 4, core: 2. Of those that a mesh axis runs over, the one named last changes fastest.
Arguments:
- orbitals: float32 [640, 12288], P('band', 'grid'), may hold values from -6 to 6
Outputs:
- corrected: float32 [640, 12288], P('band', 'grid')
All inputs are finite; a program needn't handle non-finite values.
Results may differ from a plain program's by a relative error of at most 0.0001.
Values sent between devices are 32-bit elements; how exact they have to be, the bound alone decides.
A program may use at most 64 MiB of HBM per device.

v0:
```python
import jax
import jax.numpy as jnp
from jax import lax
from jax.sharding import PartitionSpec as P


def passed_along(block, axis, distance):
    devices = range(lax.axis_size(axis))
    route = [((i - distance) % len(devices), i) for i in devices]
    return lax.ppermute(block, axis, route)


def product(left, right):
    return jnp.dot(left, right, precision=lax.Precision.HIGHEST, preferred_element_type=jnp.float32)


def shards(orbitals):
    band_count = lax.axis_size("band")
    shifts = min(4, (band_count - 1) // 2)
    points = orbitals.shape[1] * lax.axis_size("grid")
    others = []
    for distance in range(1, shifts + 1):
        others.append(passed_along(orbitals, "band", distance))
    neighbours = [orbitals] + others
    partials = [product(orbitals, other.T) for other in neighbours]
    tiles = [lax.psum(partial_value, "grid") / points for partial_value in partials]
    identity = jnp.eye(orbitals.shape[0], dtype=jnp.float32)
    fix = product(tiles[0] - identity, orbitals)
    terms = [None]
    for distance in range(1, shifts + 1):
        fix = fix + product(tiles[distance], others[distance - 1])
        terms.append(product(tiles[distance].T, orbitals))
    for distance in range(1, shifts + 1):
        fix = fix + passed_along(terms[distance], "band", -distance)
    return orbitals - 0.5 * fix


def solution(mesh):
    return jax.shard_map(
        shards,
        mesh=mesh,
        in_specs=(P("band", "grid"),),
        out_specs=P("band", "grid"),
        check_vma=False,
    )
```

profile of v0, /device:TPU:0, one launch (start us, length us, event | category | flops | bytes accessed | tf_op | source)
XLA Modules:
  0.0 122.8 jit_solution(8305146317680906826)
XLA Ops:
  6.5 0.0 copy-start
  6.5 0.0 all-reduce.3.cloned.1.call-start
  6.5 2.9 %collective-permute-start = (f32[160,1536]{1,0:T(8,128)}, f32[160,1536]{1,0:T(8,128)S(1)}, u32[]{:S(2)}, u32[]{:S(2)}) collective-permute-start(f32[160,1536]{1,0:T(8,128)} %param.1), channel_id=1, source_target_pairs={{24,0},{0,8},{8,16},{16,24},{25,1},{1,9},{9,17},{17,25},{26,2},{2,... | collective-permute-start | bytes 2949128 | tf_op jit(solution)/shard_map/ppermute | solution.py:10
  9.5 3.2 %fusion.16 = f32[160,160]{1,0:T(8,128)} fusion(f32[160,1536]{1,0:T(8,128)} %param.1), kind=kOutput, calls=%fused_computation.18 | convolution fusion | flops 471859200 | bytes 1085440 | tf_op jit(solution)/shard_map/dot_general | solution.py:14
  12.7 19.8 %collective-permute-done = f32[160,1536]{1,0:T(8,128)S(1)} collective-permute-done((f32[160,1536]{1,0:T(8,128)}, f32[160,1536]{1,0:T(8,128)S(1)}, u32[]{:S(2)}, u32[]{:S(2)}) %collective-permute-start) | collective-permute-done | bytes 983072 | tf_op jit(solution)/shard_map/ppermute | solution.py:10
  32.5 0.0 copy-done
  32.5 1.6 %fusion.17 = f32[160,160]{1,0:T(8,128)} fusion(f32[160,1536]{1,0:T(8,128)S(1)} %copy-done, f32[160,1536]{1,0:T(8,128)S(1)} %collective-permute-done), kind=kOutput, calls=%fused_computation.19 | convolution fusion | flops 471859200 | bytes 2068480 | tf_op jit(solution)/shard_map/dot_general | solution.py:14
  34.1 0.0 all-reduce.3.cloned.1.call-update
  34.1 56.1 %all-reduce.3.cloned.1.call-done = (f32[160,160]{1,0:T(8,128)}, f32[160,160]{1,0:T(8,128)}) async-done(((f32[160,160]{1,0:T(8,128)}, f32[160,160]{1,0:T(8,128)}), (f32[160,160]{1,0:T(8,128)}, f32[160,160]{1,0:T(8,128)})) %all-reduce.3.cloned.1.call-update) | async-done | bytes 204816 | tf_op jit(solution)/shard_map/psum | solution.py:26
  90.2 0.0 copy-start.2
  90.2 2.0 %fusion.7 = f32[160,1536]{1,0:T(8,128)S(1)} fusion(f32[160,1536]{1,0:T(8,128)S(1)} %copy-done, f32[160,160]{1,0:T(8,128)} %get-tuple-element.5), kind=kOutput, calls=%fused_computation.9 | convolution fusion | flops 471884800 | bytes 2068480 | tf_op jit(solution)/shard_map/dot_general | solution.py:14
  92.2 2.4 %collective-permute-start.1 = (f32[160,1536]{1,0:T(8,128)S(1)}, f32[160,1536]{1,0:T(8,128)S(1)}, u32[]{:S(2)}, u32[]{:S(2)}) collective-permute-start(f32[160,1536]{1,0:T(8,128)S(1)} %fusion.7), channel_id=1, source_target_pairs={{8,0},{16,8},{24,16},{0,24},{9,1},{17,9},{25,17},{1,25},{10,2},{18... | collective-permute-start | bytes 2949128 | tf_op jit(solution)/shard_map/ppermute | solution.py:10
  94.6 0.0 copy-done.2
  94.6 0.0 copy-start.1
  94.6 1.0 fusion.3
  95.6 18.4 %collective-permute-done.1 = f32[160,1536]{1,0:T(8,128)S(1)} collective-permute-done((f32[160,1536]{1,0:T(8,128)S(1)}, f32[160,1536]{1,0:T(8,128)S(1)}, u32[]{:S(2)}, u32[]{:S(2)}) %collective-permute-start.1) | collective-permute-done | bytes 983072 | tf_op jit(solution)/shard_map/ppermute | solution.py:10
  114.0 0.0 copy-done.1
  114.0 2.0 %fusion.2 = f32[160,1536]{1,0:T(8,128)} fusion(f32[160,1536]{1,0:T(8,128)S(1)} %copy-done, f32[160,1536]{1,0:T(8,128)S(1)} %collective-permute-done.1, f32[160,1536]{1,0:T(8,128)S(1)} %fusion.3, f32[160,1536]{1,0:T(8,128)S(1)} %collective-permute-done, f32[160,160]{1,0:T(8,128)S(1)} %copy-done.1), kind=kOutput, calls=%fused_computation.3 | convolution fusion | flops 472867840 | bytes 5017600 | tf_op jit(solution)/shard_map/dot_general | solution.py:14
Async XLA Ops:
  6.5 25.9 %copy-start = (f32[160,1536]{1,0:T(8,128)S(1)}, f32[160,1536]{1,0:T(8,128)}, u32[]{:S(2)}) copy-start(f32[160,1536]{1,0:T(8,128)} %param.1) | copy-start | bytes 2949124
  6.5 83.7 %all-reduce.3.cloned.1.call-start = ((), (), s32[]{:S(2)}) async-start(), calls=%async_computation | async-start | bytes 655360 | tf_op jit(solution)/shard_map/psum | solution.py:26
  6.5 25.9 %collective-permute-start = (f32[160,1536]{1,0:T(8,128)}, f32[160,1536]{1,0:T(8,128)S(1)}, u32[]{:S(2)}, u32[]{:S(2)}) collective-permute-start(f32[160,1536]{1,0:T(8,128)} %param.1), channel_id=1, source_target_pairs={{24,0},{0,8},{8,16},{16,24},{25,1},{1,9},{9,17},{17,25},{26,2},{2,... | collective-permute-start | bytes 2949128 | tf_op jit(solution)/shard_map/ppermute | solution.py:10
  90.2 4.4 %copy-start.2 = (f32[160,160]{1,0:T(8,128)S(1)}, f32[160,160]{1,0:T(8,128)}, u32[]{:S(2)}) copy-start(f32[160,160]{1,0:T(8,128)} %get-tuple-element.6) | copy-start | bytes 307204
  92.2 21.8 %collective-permute-start.1 = (f32[160,1536]{1,0:T(8,128)S(1)}, f32[160,1536]{1,0:T(8,128)S(1)}, u32[]{:S(2)}, u32[]{:S(2)}) collective-permute-start(f32[160,1536]{1,0:T(8,128)S(1)} %fusion.7), channel_id=1, source_target_pairs={{8,0},{16,8},{24,16},{0,24},{9,1},{17,9},{25,17},{1,25},{10,2},{18... | collective-permute-start | bytes 2949128 | tf_op jit(solution)/shard_map/ppermute | solution.py:10
  94.6 19.4 %copy-start.1 = (f32[160,160]{1,0:T(8,128)S(1)}, f32[160,160]{1,0:T(8,128)}, u32[]{:S(2)}) copy-start(f32[160,160]{1,0:T(8,128)} %get-tuple-element.5) | copy-start | bytes 307204
Sparse Core Ops, SparseCore 0:
  34.2 55.9 all-reduce.2
where the time goes:
time: 123 us
  waiting for transfers between devices  94.3 us (77%)
  between operations  13.4 us (11%)
  matrix products  9.73 us (8%)
  starting transfers between devices  5.37 us (4%)
    psum x1, waiting for transfers between devices, shards(): lax.psum(partial_value, 'grid') / points  56.1 us
    ppermute x2, waiting for transfers between devices, passed_along(): return lax.ppermute(block, axis, route)  38.2 us
    dot_general x5, matrix products, product(): jnp.dot(left, right, precision=lax.Precision.HIGHEST, preferred_element_t...  9.73 us
    ppermute x2, starting transfers between devices, passed_along(): return lax.ppermute(block, axis, route)  5.37 us
  transfers between devices with their start and end apart: 3, of which 3 were waited for; matrix products, arithmetic and copies ran while one was open for 3% of the time, Pallas kernels for 0%

commit v1 on v0

--- a/solution.py
+++ b/solution.py
@@ -1,7 +1,15 @@
+import functools
+
 import jax
 import jax.numpy as jnp
 from jax import lax
+from jax.experimental import pallas as pl
+from jax.experimental.pallas import tpu as pltpu
 from jax.sharding import PartitionSpec as P
+
+MESH = pl.DeviceIdType.MESH
+NT = (((1,), (1,)), ((), ()))
+NN = (((1,), (0,)), ((), ()))
 
 
 def passed_along(block, axis, distance):
@@ -14,7 +22,7 @@
     return jnp.dot(left, right, precision=lax.Precision.HIGHEST, preferred_element_type=jnp.float32)
 
 
-def shards(orbitals):
+def general_shards(orbitals):
     band_count = lax.axis_size("band")
     shifts = min(4, (band_count - 1) // 2)
     points = orbitals.shape[1] * lax.axis_size("grid")
@@ -35,6 +43,291 @@
     return orbitals - 0.5 * fix
 
 
+def split(a):
+    hi = a.astype(jnp.bfloat16)
+    return hi, (a - hi.astype(jnp.float32)).astype(jnp.bfloat16)
+
+
+def mm(a, b, dims):
+    dot = functools.partial(lax.dot_general, dimension_numbers=dims, preferred_element_type=jnp.float32)
+    return dot(a[0], b[0]) + (dot(a[0], b[1]) + dot(a[1], b[0]))
+
+
+def kernel(
+    nr, width, depth, x_ref, o_ref,
+    blocks, dpart, drs, dred, dfull, tpart, tcore, trs, tred, tpair, tfull, fix,
+    own_sem, xs, xr, ys, yr, drss, drsr, dags, dagr, cs, cr, rss, rsr, ps, pr, ags, agr, fs, fr, os,
+):
+    bd, cols = x_ref.shape
+    nz = nr // 2
+    points = cols * nr
+    half = cols // 2
+    n = cols // width
+    nh = n // 2
+    g = lax.axis_index("band")
+    r = lax.axis_index("grid")
+    z, core = r // 2, r % 2
+    par = g % 2
+    xn, yn, dn = g + 1 - 2 * par, (g + 2) % 4, 3 - g
+    mate = z * 2 + (1 - core)
+    partner = xn * (1 - core) + dn * core
+
+    own_copy = pltpu.make_async_copy(x_ref, blocks.at[pl.ds(0, bd)], own_sem)
+    own_copy.start()
+
+    barrier = pltpu.get_barrier_semaphore()
+    for peer in (xn, yn, dn):
+        pl.semaphore_signal(barrier, inc=1, device_id={"band": peer}, device_id_type=MESH)
+    for k in range(1, nr):
+        pl.semaphore_signal(barrier, inc=1, device_id={"grid": (r + k) % nr}, device_id_type=MESH)
+    pl.semaphore_wait(barrier, 3 + nr - 1)
+
+    def columns(c, parity):
+        start = parity * half + c * width
+        start = lax.rem(start, cols)
+        return pl.ds(pl.multiple_of(start, 128), width)
+
+    def remote(src, dst, send, recv, where):
+        return pltpu.make_async_remote_copy(
+            src_ref=src, dst_ref=dst, send_sem=send, recv_sem=recv, device_id=where, device_id_type=MESH)
+
+    def x_send(c):
+        at = columns(c, 1 - par)
+        return remote(x_ref.at[:, at], blocks.at[pl.ds(bd, bd), at], xs.at[c], xr.at[c], {"band": xn})
+
+    def x_recv(c):
+        at = columns(c, par)
+        return remote(x_ref.at[:, at], blocks.at[pl.ds(bd, bd), at], xs.at[c], xr.at[c], {"band": xn})
+
+    def y_copy(c):
+        at = columns(c, par)
+        return remote(blocks.at[pl.ds(bd, bd), at], blocks.at[pl.ds(2 * bd, bd), at], ys.at[c], yr.at[c], {"band": yn})
+
+    for c in range(min(depth, n)):
+        x_send(c).start()
+
+    own_copy.wait()
+
+    def step_x(c):
+        x_recv(c).wait_recv()
+        y_copy(c).start()
+        x_send(c).wait_send()
+        if c + depth < n:
+            x_send(c + depth).start()
+
+    mine = split(blocks[pl.ds(0, bd), :])
+    own_tile = mm(mine, mine, NT)
+    rows = bd // nr
+    for j in range(nr):
+        dpart[j] = own_tile[j * rows:(j + 1) * rows]
+
+    def drs_copy(k):
+        return remote(dpart.at[(r + k) % nr], drs.at[k - 1], drss.at[k - 1], drsr.at[k - 1], {"grid": (r + k) % nr})
+
+    def dag_copy(k):
+        return remote(dred, dfull.at[r], dags.at[k - 1], dagr.at[k - 1], {"grid": (r + k) % nr})
+
+    def dag_arrival(k):
+        return remote(dred, dfull.at[(r + nr - k) % nr], dags.at[k - 1], dagr.at[k - 1], {"grid": (r + k) % nr})
+
+    for k in range(1, nr):
+        drs_copy(k).start()
+
+    def add_tile(which, c):
+        at = columns(c, par)
+        a = split(blocks[pl.ds(0, bd), at])
+        b = split(blocks[pl.ds((1 + which) * bd, bd), at])
+
+        @pl.when(par == 0)
+        def _():
+            value = mm(a, b, NT).reshape(nz, bd // nz, bd)
+            tpart[which] = value if c == 0 else tpart[which] + value
+
+        @pl.when(par == 1)
+        def _():
+            value = mm(b, a, NT).reshape(nz, bd // nz, bd)
+            tpart[which] = value if c == 0 else tpart[which] + value
+
+    for c in range(nh):
+        step_x(c)
+        add_tile(0, c)
+        if c >= 1:
+            y_copy(c - 1).wait_recv()
+            add_tile(1, c - 1)
+        if c == 1:
+            for k in range(1, nr):
+                drs_copy(k).wait_recv()
+            total = dpart[r]
+            for k in range(1, nr):
+                total = total + drs[k - 1]
+            dred[...] = total
+            dfull[r] = total
+            for k in range(1, nr):
+                dag_copy(k).start()
+
+    core_copy = remote(tpart.at[1 - core], tcore, cs, cr, {"grid": mate})
+
+    @pl.when(core == 1)
+    def _():
+        core_copy.start()
+
+    step_x(nh)
+    y_copy(nh - 1).wait_recv()
+    add_tile(1, nh - 1)
+
+    @pl.when(core == 0)
+    def _():
+        core_copy.start()
+
+    def other_z(k):
+        return lax.rem(z + k, nz)
+
+    def rs_copy(k):
+        return remote(tcore.at[other_z(k)], trs.at[k - 1], rss.at[k - 1], rsr.at[k - 1], {"grid": other_z(k) * 2 + core})
+
+    core_copy.wait()
+    tcore[...] = tcore[...] + tpart[core]
+    for k in range(1, nz):
+        rs_copy(k).start()
+    step_x(nh + 1)
+    step_x(nh + 2)
+    for k in range(1, nz):
+        rs_copy(k).wait_recv()
+    total = tcore[z]
+    for k in range(1, nz):
+        total = total + trs[k - 1]
+    tred[...] = total
+    pair_copy = remote(tred, tpair, ps, pr, {"band": partner})
+    pair_copy.start()
+    for c in range(nh + 3, n - 1):
+        step_x(c)
+    pair_copy.wait()
+    total = tred[...] + tpair[...]
+    tfull[core, z] = total
+
+    def ag_copy(k):
+        return remote(tfull.at[core, z], tfull.at[core, z], ags.at[k - 1], agr.at[k - 1], {"grid": other_z(k) * 2 + core})
+
+    def ag_arrival(k):
+        at = tfull.at[core, lax.rem(z + nz - k, nz)]
+        return remote(at, at, ags.at[k - 1], agr.at[k - 1], {"grid": other_z(k) * 2 + core})
+
+    def mate_copy(k):
+        at = tfull.at[core, lax.rem(z + nz - k, nz)]
+        return remote(at, at, fs.at[k], fr.at[k], {"grid": mate})
+
+    def mate_arrival(k):
+        at = tfull.at[1 - core, lax.rem(z + nz - k, nz)]
+        return remote(at, at, fs.at[k], fr.at[k], {"grid": mate})
+
+    for k in range(1, nz):
+        ag_copy(k).start()
+    mate_copy(0).start()
+    step_x(n - 1)
+
+    for k in range(1, nr):
+        dag_arrival(k).wait_recv()
+    scale = -0.5 / points
+    own_w = split(jnp.concatenate([dfull[j] for j in range(nr)], axis=0) * scale)
+    wide = 2 * width
+    for t in range(cols // wide):
+        at = pl.ds(t * wide, wide)
+        a = blocks[pl.ds(0, bd), at]
+        fix[:, at] = 1.5 * a + mm(own_w, split(a), NN)
+
+    for k in range(1, nz):
+        ag_arrival(k).wait_recv()
+        mate_copy(k).start()
+    for c in range(nh, n):
+        y_copy(c).wait_recv()
+    for k in range(nz):
+        mate_arrival(k).wait_recv()
+
+    @pl.when(par == 1)
+    def _():
+        for which in range(2):
+            tpart[which] = tfull[which].reshape(bd, bd).T.reshape(nz, bd // nz, bd)
+
+    @pl.when(par == 0)
+    def _():
+        for which in range(2):
+            tpart[which] = tfull[which]
+
+    w0 = split(tpart[0].reshape(bd, bd) * scale)
+    w1 = split(tpart[1].reshape(bd, bd) * scale)
+    outs = []
+    for t in range(cols // wide):
+        at = pl.ds(t * wide, wide)
+        b0 = split(blocks[pl.ds(bd, bd), at])
+        b1 = split(blocks[pl.ds(2 * bd, bd), at])
+        fix[:, at] = fix[:, at] + (mm(w0, b0, NN) + mm(w1, b1, NN))
+        outs.append(pltpu.make_async_copy(fix.at[:, at], o_ref.at[:, at], os.at[t]))
+        outs[-1].start()
+
+    for c in range(n):
+        y_copy(c).wait_send()
+    for k in range(1, nr):
+        drs_copy(k).wait_send()
+        dag_copy(k).wait_send()
+    for k in range(1, nz):
+        rs_copy(k).wait_send()
+        ag_copy(k).wait_send()
+    for k in range(nz):
+        mate_copy(k).wait_send()
+    for copy in outs:
+        copy.wait()
+
+
+def paired_shards(orbitals):
+    bd, cols = orbitals.shape
+    nr = lax.axis_size("grid")
+    nz = nr // 2
+    width = 128
+    n = cols // width
+    f32 = jnp.float32
+    dma = pltpu.SemaphoreType.DMA
+    rows = bd // nr
+    part = bd // nz
+    return pl.pallas_call(
+        functools.partial(kernel, nr, width, 3),
+        out_shape=jax.ShapeDtypeStruct((bd, cols), f32),
+        in_specs=[pl.BlockSpec(memory_space=pl.ANY)],
+        out_specs=pl.BlockSpec(memory_space=pl.ANY),
+        scratch_shapes=[
+            pltpu.VMEM((3 * bd, cols), f32),
+            pltpu.VMEM((nr, rows, bd), f32),
+            pltpu.VMEM((nr - 1, rows, bd), f32),
+            pltpu.VMEM((rows, bd), f32),
+            pltpu.VMEM((nr, rows, bd), f32),
+            pltpu.VMEM((2, nz, part, bd), f32),
+            pltpu.VMEM((nz, part, bd), f32),
+            pltpu.VMEM((nz - 1, part, bd), f32),
+            pltpu.VMEM((part, bd), f32),
+            pltpu.VMEM((part, bd), f32),
+            pltpu.VMEM((2, nz, part, bd), f32),
+            pltpu.VMEM((bd, cols), f32),
+            dma, dma((n,)), dma((n,)), dma((n,)), dma((n,)),
+            dma((nr - 1,)), dma((nr - 1,)), dma((nr - 1,)), dma((nr - 1,)),
+            dma, dma, dma((nz - 1,)), dma((nz - 1,)), dma, dma,
+            dma((nz - 1,)), dma((nz - 1,)), dma((nz,)), dma((nz,)),
+            dma((n // 2,)),
+        ],
+        compiler_params=pltpu.CompilerParams(
+            collective_id=0, has_side_effects=True, vmem_limit_bytes=32 * 1024 * 1024),
+        cost_estimate=pl.CostEstimate(
+            flops=12 * bd * bd * cols, bytes_accessed=8 * bd * cols, transcendentals=0),
+    )(orbitals)
+
+
+def shards(orbitals):
+    bd, cols = orbitals.shape
+    nr = lax.axis_size("grid")
+    fits = nr % 2 == 0 and nr >= 4 and bd % (4 * nr) == 0 and cols % 256 == 0 and cols >= 2048 // 2
+    if lax.axis_size("band") == 4 and fits:
+        return paired_shards(orbitals)
+    return general_shards(orbitals)
+
+
 def solution(mesh):
     return jax.shard_map(
         shards,

time: 123 us -> 44.7 us (0.36)
  the two profiles are of different devices: /device:TPU:0 before, /device:TPU:1 now
where the time goes in v1:
time: 44.7 us; the launch traced here: 44.6 us
  Pallas kernels  42.4 us (95%)
  local copies, waits for them, and re-layouts  2.15 us (5%)
    pallas_call x1, Pallas kernels, paired_shards(): pl.pallas_call(functools.partial(kernel, nr, width, 3), out_shape=jax.Sha...  42.4 us
    unnamed x3, local copies, waits for them, and re-layouts  2.15 us

profile of v1, /device:TPU:1, one launch (start us, length us, event | category | flops | bytes accessed | tf_op | source)
XLA Modules:
  0.0 44.6 jit_solution(8728646859507954175)
XLA Ops:
  0.0 0.0 copy-start
  0.0 1.2 %copy-done = f32[160,1536]{1,0:T(8,128)S(1)} copy-done((f32[160,1536]{1,0:T(8,128)S(1)}, f32[160,1536]{1,0:T(8,128)}, u32[]{:S(2)}) %copy-start) | copy-done | bytes 983064
  1.2 42.4 %shard_map.17 = f32[160,1536]{1,0:T(8,128)S(1)} custom-call(f32[160,1536]{1,0:T(8,128)S(1)} %copy-done), custom_call_target="tpu_custom_call" | custom-call | flops 471859200 | bytes 1966080 | tf_op jit(solution)/shard_map/pallas_call | solution.py:291
  43.6 0.9 %copy.3 = f32[160,1536]{1,0:T(8,128)} copy(f32[160,1536]{1,0:T(8,128)S(1)} %shard_map.17) | data formatting | bytes 1966080
Async XLA Ops:
  0.0 1.2 %copy-start = (f32[160,1536]{1,0:T(8,128)S(1)}, f32[160,1536]{1,0:T(8,128)}, u32[]{:S(2)}) copy-start(f32[160,1536]{1,0:T(8,128)} %x_ref.1) | copy-start | bytes 2949124

commit v2 on v1

--- a/solution.py
+++ b/solution.py
@@ -55,8 +55,8 @@
 
 def kernel(
     nr, width, depth, x_ref, o_ref,
-    blocks, dpart, drs, dred, dfull, tpart, tcore, trs, tred, tpair, tfull, fix,
-    own_sem, xs, xr, ys, yr, drss, drsr, dags, dagr, cs, cr, rss, rsr, ps, pr, ags, agr, fs, fr, os,
+    blocks, dpart, dcore, drs, dred, dfull, tpart, tcore, trs, tred, tpair, tfull, fix,
+    own_sem, xs, xr, ys, yr, dcs, dcr, drss, drsr, dags, dagr, cs, cr, rss, rsr, ps, pr, ags, agr, fs, fr, os,
 ):
     bd, cols = x_ref.shape
     nz = nr // 2
@@ -78,9 +78,11 @@
     barrier = pltpu.get_barrier_semaphore()
     for peer in (xn, yn, dn):
         pl.semaphore_signal(barrier, inc=1, device_id={"band": peer}, device_id_type=MESH)
-    for k in range(1, nr):
-        pl.semaphore_signal(barrier, inc=1, device_id={"grid": (r + k) % nr}, device_id_type=MESH)
-    pl.semaphore_wait(barrier, 3 + nr - 1)
+    pl.semaphore_signal(barrier, inc=1, device_id={"grid": mate}, device_id_type=MESH)
+    for k in range(1, nz):
+        pl.semaphore_signal(
+            barrier, inc=1, device_id={"grid": lax.rem(z + k, nz) * 2 + core}, device_id_type=MESH)
+    pl.semaphore_wait(barrier, 4 + nz - 1)
 
     def columns(c, parity):
         start = parity * half + c * width
@@ -116,22 +118,25 @@
             x_send(c + depth).start()
 
     mine = split(blocks[pl.ds(0, bd), :])
-    own_tile = mm(mine, mine, NT)
-    rows = bd // nr
-    for j in range(nr):
-        dpart[j] = own_tile[j * rows:(j + 1) * rows]
+    dpart[...] = mm(mine, mine, NT).reshape(nz, bd // nz, bd)
+
+    def other_z(k):
+        return lax.rem(z + k, nz)
+
+    def to_z(k):
+        return {"grid": other_z(k) * 2 + core}
 
     def drs_copy(k):
-        return remote(dpart.at[(r + k) % nr], drs.at[k - 1], drss.at[k - 1], drsr.at[k - 1], {"grid": (r + k) % nr})
+        return remote(dcore.at[other_z(k)], drs.at[k - 1], drss.at[k - 1], drsr.at[k - 1], to_z(k))
 
     def dag_copy(k):
-        return remote(dred, dfull.at[r], dags.at[k - 1], dagr.at[k - 1], {"grid": (r + k) % nr})
+        return remote(dred, dfull.at[z], dags.at[k - 1], dagr.at[k - 1], to_z(k))
 
     def dag_arrival(k):
-        return remote(dred, dfull.at[(r + nr - k) % nr], dags.at[k - 1], dagr.at[k - 1], {"grid": (r + k) % nr})
-
-    for k in range(1, nr):
-        drs_copy(k).start()
+        return remote(dred, dfull.at[lax.rem(z + nz - k, nz)], dags.at[k - 1], dagr.at[k - 1], to_z(k))
+
+    dcore_copy = remote(dpart, dcore, dcs, dcr, {"grid": mate})
+    dcore_copy.start()
 
     def add_tile(which, c):
         at = columns(c, par)
@@ -154,122 +159,143 @@
         if c >= 1:
             y_copy(c - 1).wait_recv()
             add_tile(1, c - 1)
-        if c == 1:
-            for k in range(1, nr):
+        if c == 0:
+            dcore_copy.wait()
+            dcore[...] = dcore[...] + dpart[...]
+            for k in range(1, nz):
+                drs_copy(k).start()
+        if c == 2:
+            for k in range(1, nz):
                 drs_copy(k).wait_recv()
-            total = dpart[r]
-            for k in range(1, nr):
+            total = dcore[z]
+            for k in range(1, nz):
                 total = total + drs[k - 1]
             dred[...] = total
-            dfull[r] = total
-            for k in range(1, nr):
+            dfull[z] = total
+            for k in range(1, nz):
                 dag_copy(k).start()
 
     core_copy = remote(tpart.at[1 - core], tcore, cs, cr, {"grid": mate})
-
-    @pl.when(core == 1)
-    def _():
-        core_copy.start()
-
+    pair_copy = remote(tred, tpair, ps, pr, {"band": partner})
+
+    def rs_copy(k):
+        return remote(tcore.at[other_z(k)], trs.at[k - 1], rss.at[k - 1], rsr.at[k - 1], to_z(k))
+
+    def ag_copy(k):
+        return remote(tfull.at[core, z], tfull.at[core, z], ags.at[k - 1], agr.at[k - 1], {"grid": other_z(k) * 2 + core})
+
+    def ag_arrival(k):
+        at = tfull.at[core, lax.rem(z + nz - k, nz)]
+        return remote(at, at, ags.at[k - 1], agr.at[k - 1], {"grid": other_z(k) * 2 + core})
+
+    def mate_copy(k):
+        at = tfull.at[core, lax.rem(z + nz - k, nz)]
+        return remote(at, at, fs.at[k], fr.at[k], {"grid": mate})
+
+    def mate_arrival(k):
+        at = tfull.at[1 - core, lax.rem(z + nz - k, nz)]
+        return remote(at, at, fs.at[k], fr.at[k], {"grid": mate})
+
+    def on(which, stage):
+        @pl.when(core == which)
+        def _():
+            stage()
+
+    def sum_cores():
+        core_copy.wait_recv()
+        tcore[...] = tcore[...] + tpart[core]
+        for k in range(1, nz):
+            rs_copy(k).start()
+
+    def sum_z():
+        for k in range(1, nz):
+            rs_copy(k).wait_recv()
+        total = tcore[z]
+        for k in range(1, nz):
+            total = total + trs[k - 1]
+        tred[...] = total
+        pair_copy.start()
+
+    def sum_pair():
+        pair_copy.wait_recv()
+        tfull[core, z] = tred[...] + tpair[...]
+        for k in range(1, nz):
+            ag_copy(k).start()
+        mate_copy(0).start()
+
+    def pass_on():
+        for k in range(1, nz):
+            ag_arrival(k).wait_recv()
+            mate_copy(k).start()
+
+    def from_mate():
+        for k in range(nz):
+            mate_arrival(k).wait_recv()
+
+    on(1, core_copy.start)
+    on(0, sum_cores)
     step_x(nh)
     y_copy(nh - 1).wait_recv()
     add_tile(1, nh - 1)
-
-    @pl.when(core == 0)
-    def _():
-        core_copy.start()
-
-    def other_z(k):
-        return lax.rem(z + k, nz)
-
-    def rs_copy(k):
-        return remote(tcore.at[other_z(k)], trs.at[k - 1], rss.at[k - 1], rsr.at[k - 1], {"grid": other_z(k) * 2 + core})
-
-    core_copy.wait()
-    tcore[...] = tcore[...] + tpart[core]
+    on(0, core_copy.start)
+    on(1, sum_cores)
+    on(0, sum_z)
+    for c in range(nh + 1, nh + 4):
+        if c < n:
+            step_x(c)
+    on(0, sum_pair)
+    for c in range(nh + 4, n - 1):
+        step_x(c)
+    on(1, sum_z)
+    for c in range(max(n - 1, nh + 4), n):
+        step_x(c)
+    on(1, sum_pair)
+
     for k in range(1, nz):
-        rs_copy(k).start()
-    step_x(nh + 1)
-    step_x(nh + 2)
-    for k in range(1, nz):
-        rs_copy(k).wait_recv()
-    total = tcore[z]
-    for k in range(1, nz):
-        total = total + trs[k - 1]
-    tred[...] = total
-    pair_copy = remote(tred, tpair, ps, pr, {"band": partner})
-    pair_copy.start()
-    for c in range(nh + 3, n - 1):
-        step_x(c)
-    pair_copy.wait()
-    total = tred[...] + tpair[...]
-    tfull[core, z] = total
-
-    def ag_copy(k):
-        return remote(tfull.at[core, z], tfull.at[core, z], ags.at[k - 1], agr.at[k - 1], {"grid": other_z(k) * 2 + core})
-
-    def ag_arrival(k):
-        at = tfull.at[core, lax.rem(z + nz - k, nz)]
-        return remote(at, at, ags.at[k - 1], agr.at[k - 1], {"grid": other_z(k) * 2 + core})
-
-    def mate_copy(k):
-        at = tfull.at[core, lax.rem(z + nz - k, nz)]
-        return remote(at, at, fs.at[k], fr.at[k], {"grid": mate})
-
-    def mate_arrival(k):
-        at = tfull.at[1 - core, lax.rem(z + nz - k, nz)]
-        return remote(at, at, fs.at[k], fr.at[k], {"grid": mate})
-
-    for k in range(1, nz):
-        ag_copy(k).start()
-    mate_copy(0).start()
-    step_x(n - 1)
-
-    for k in range(1, nr):
         dag_arrival(k).wait_recv()
     scale = -0.5 / points
-    own_w = split(jnp.concatenate([dfull[j] for j in range(nr)], axis=0) * scale)
     wide = 2 * width
-    for t in range(cols // wide):
-        at = pl.ds(t * wide, wide)
+    steps = [pl.ds(t * wide, wide) for t in range(cols // wide)]
+    on(0, pass_on)
+    own_w = split(dfull[...].reshape(bd, bd) * scale)
+    for at in steps:
         a = blocks[pl.ds(0, bd), at]
         fix[:, at] = 1.5 * a + mm(own_w, split(a), NN)
-
-    for k in range(1, nz):
-        ag_arrival(k).wait_recv()
-        mate_copy(k).start()
+    core_copy.wait_send()
+
+    def weights(which):
+        @pl.when(par == 1)
+        def _():
+            tpart[which] = tfull[which].reshape(bd, bd).T.reshape(nz, bd // nz, bd)
+
+        @pl.when(par == 0)
+        def _():
+            tpart[which] = tfull[which]
+
+        return split(tpart[which].reshape(bd, bd) * scale)
+
+    on(1, from_mate)
+    w0 = weights(0)
+    for at in steps:
+        fix[:, at] = fix[:, at] + mm(w0, split(blocks[pl.ds(bd, bd), at]), NN)
+
+    on(1, pass_on)
     for c in range(nh, n):
         y_copy(c).wait_recv()
-    for k in range(nz):
-        mate_arrival(k).wait_recv()
-
-    @pl.when(par == 1)
-    def _():
-        for which in range(2):
-            tpart[which] = tfull[which].reshape(bd, bd).T.reshape(nz, bd // nz, bd)
-
-    @pl.when(par == 0)
-    def _():
-        for which in range(2):
-            tpart[which] = tfull[which]
-
-    w0 = split(tpart[0].reshape(bd, bd) * scale)
-    w1 = split(tpart[1].reshape(bd, bd) * scale)
+    on(0, from_mate)
+    w1 = weights(1)
     outs = []
-    for t in range(cols // wide):
-        at = pl.ds(t * wide, wide)
-        b0 = split(blocks[pl.ds(bd, bd), at])
-        b1 = split(blocks[pl.ds(2 * bd, bd), at])
-        fix[:, at] = fix[:, at] + (mm(w0, b0, NN) + mm(w1, b1, NN))
+    for t, at in enumerate(steps):
+        fix[:, at] = fix[:, at] + mm(w1, split(blocks[pl.ds(2 * bd, bd), at]), NN)
         outs.append(pltpu.make_async_copy(fix.at[:, at], o_ref.at[:, at], os.at[t]))
         outs[-1].start()
 
     for c in range(n):
         y_copy(c).wait_send()
-    for k in range(1, nr):
+    pair_copy.wait_send()
+    for k in range(1, nz):
         drs_copy(k).wait_send()
         dag_copy(k).wait_send()
-    for k in range(1, nz):
         rs_copy(k).wait_send()
         ag_copy(k).wait_send()
     for k in range(nz):
@@ -286,7 +312,6 @@
     n = cols // width
     f32 = jnp.float32
     dma = pltpu.SemaphoreType.DMA
-    rows = bd // nr
     part = bd // nz
     return pl.pallas_call(
         functools.partial(kernel, nr, width, 3),
@@ -295,10 +320,11 @@
         out_specs=pl.BlockSpec(memory_space=pl.ANY),
         scratch_shapes=[
             pltpu.VMEM((3 * bd, cols), f32),
-            pltpu.VMEM((nr, rows, bd), f32),
-            pltpu.VMEM((nr - 1, rows, bd), f32),
-            pltpu.VMEM((rows, bd), f32),
-            pltpu.VMEM((nr, rows, bd), f32),
+            pltpu.VMEM((nz, part, bd), f32),
+            pltpu.VMEM((nz, part, bd), f32),
+            pltpu.VMEM((nz - 1, part, bd), f32),
+            pltpu.VMEM((part, bd), f32),
+            pltpu.VMEM((nz, part, bd), f32),
             pltpu.VMEM((2, nz, part, bd), f32),
             pltpu.VMEM((nz, part, bd), f32),
             pltpu.VMEM((nz - 1, part, bd), f32),
@@ -307,13 +333,13 @@
             pltpu.VMEM((2, nz, part, bd), f32),
             pltpu.VMEM((bd, cols), f32),
             dma, dma((n,)), dma((n,)), dma((n,)), dma((n,)),
-            dma((nr - 1,)), dma((nr - 1,)), dma((nr - 1,)), dma((nr - 1,)),
+            dma, dma, dma((nz - 1,)), dma((nz - 1,)), dma((nz - 1,)), dma((nz - 1,)),
             dma, dma, dma((nz - 1,)), dma((nz - 1,)), dma, dma,
             dma((nz - 1,)), dma((nz - 1,)), dma((nz,)), dma((nz,)),
             dma((n // 2,)),
         ],
         compiler_params=pltpu.CompilerParams(
-            collective_id=0, has_side_effects=True, vmem_limit_bytes=32 * 1024 * 1024),
+            collective_id=0, has_side_effects=True, vmem_limit_bytes=60 * 1024 * 1024),
         cost_estimate=pl.CostEstimate(
             flops=12 * bd * bd * cols, bytes_accessed=8 * bd * cols, transcendentals=0),
     )(orbitals)

time: 44.7 us -> 41.8 us (0.935)
  the two profiles are of different devices: /device:TPU:1 before, /device:TPU:0 now
where the time goes in v2:
time: 41.8 us; the launch traced here: 41.7 us
  Pallas kernels  39.5 us (94%)
  local copies, waits for them, and re-layouts  2.21 us (5%)
    pallas_call x1, Pallas kernels, paired_shards(): pl.pallas_call(functools.partial(kernel, nr, width, 3), out_shape=jax.Sha...  39.5 us
    unnamed x1, local copies, waits for them, and re-layouts  2.21 us

profile of v2, /device:TPU:0, one launch (start us, length us, event | category | flops | bytes accessed | tf_op | source)
XLA Modules:
  0.0 41.7 jit_solution(1211250180989084614)
XLA Ops:
  0.0 39.5 %shard_map.17 = f32[160,1536]{1,0:T(8,128)} custom-call(f32[160,1536]{1,0:T(8,128)} %x_ref.1), custom_call_target="tpu_custom_call" | custom-call | flops 471859200 | bytes 1966080 | tf_op jit(solution)/shard_map/pallas_call | solution.py:316
  39.5 2.2 %copy.3 = f32[160,1536]{1,0:T(8,128)} copy(f32[160,1536]{1,0:T(8,128)} %shard_map.17) | data formatting | bytes 1966080

commit v3 on v2

--- a/solution.py
+++ b/solution.py
@@ -339,7 +339,7 @@
             dma((n // 2,)),
         ],
         compiler_params=pltpu.CompilerParams(
-            collective_id=0, has_side_effects=True, vmem_limit_bytes=60 * 1024 * 1024),
+            collective_id=0, has_side_effects=True, vmem_limit_bytes=105 * 512 * 1024),
         cost_estimate=pl.CostEstimate(
             flops=12 * bd * bd * cols, bytes_accessed=8 * bd * cols, transcendentals=0),
     )(orbitals)

time: 41.8 us -> 41 us (0.981)
  local copies, waits for them, and re-layouts: 2.21 us -> 0.95 us
    unnamed x1, local copies, waits for them, and re-layouts: 2.21 us -> 0.95 us
    pallas_call x1, Pallas kernels: 39.5 us -> 39.9 us  [paired_shards(): pl.pallas_call(functools.partial(kernel, nr, width, 3), out_shape=jax.Sha...]
where the time goes in v3:
time: 41 us; the launch traced here: 40.9 us
  Pallas kernels  39.9 us (97%)
  local copies, waits for them, and re-layouts  0.95 us (2%)
    pallas_call x1, Pallas kernels, paired_shards(): pl.pallas_call(functools.partial(kernel, nr, width, 3), out_shape=jax.Sha...  39.9 us
    unnamed x1, local copies, waits for them, and re-layouts  0.95 us

profile of v3, /device:TPU:0, one launch (start us, length us, event | category | flops | bytes accessed | tf_op | source)
XLA Modules:
  0.0 40.9 jit_solution(14054950370418777923)
XLA Ops:
  0.0 39.9 %shard_map.17 = f32[160,1536]{1,0:T(8,128)S(1)} custom-call(f32[160,1536]{1,0:T(8,128)} %x_ref.1), custom_call_target="tpu_custom_call" | custom-call | flops 471859200 | bytes 1966080 | tf_op jit(solution)/shard_map/pallas_call | solution.py:316
  39.9 0.9 %copy.3 = f32[160,1536]{1,0:T(8,128)} copy(f32[160,1536]{1,0:T(8,128)S(1)} %shard_map.17) | data formatting | bytes 1966080

commit v4 on v3

--- a/solution.py
+++ b/solution.py
@@ -76,12 +76,12 @@
     own_copy.start()
 
     barrier = pltpu.get_barrier_semaphore()
-    for peer in (xn, yn, dn):
-        pl.semaphore_signal(barrier, inc=1, device_id={"band": peer}, device_id_type=MESH)
-    pl.semaphore_signal(barrier, inc=1, device_id={"grid": mate}, device_id_type=MESH)
     for k in range(1, nz):
         pl.semaphore_signal(
             barrier, inc=1, device_id={"grid": lax.rem(z + k, nz) * 2 + core}, device_id_type=MESH)
+    for peer in (dn, yn, xn):
+        pl.semaphore_signal(barrier, inc=1, device_id={"band": peer}, device_id_type=MESH)
+    pl.semaphore_signal(barrier, inc=1, device_id={"grid": mate}, device_id_type=MESH)
     pl.semaphore_wait(barrier, 4 + nz - 1)
 
     def columns(c, parity):

time: 41 us -> 41 us (level)
  no operation moved by 1% of the time
where the time goes in v4:
time: 41 us; the launch traced here: 40.9 us
  Pallas kernels  39.9 us (97%)
  local copies, waits for them, and re-layouts  0.95 us (2%)
    pallas_call x1, Pallas kernels, paired_shards(): pl.pallas_call(functools.partial(kernel, nr, width, 3), out_shape=jax.Sha...  39.9 us
    unnamed x1, local copies, waits for them, and re-layouts  0.95 us

profile of v4, /device:TPU:0, one launch (start us, length us, event | category | flops | bytes accessed | tf_op | source)
XLA Modules:
  0.0 40.9 jit_solution(3007113997821564595)
XLA Ops:
  0.0 39.9 %shard_map.17 = f32[160,1536]{1,0:T(8,128)S(1)} custom-call(f32[160,1536]{1,0:T(8,128)} %x_ref.1), custom_call_target="tpu_custom_call" | custom-call | flops 471859200 | bytes 1966080 | tf_op jit(solution)/shard_map/pallas_call | solution.py:316
  39.9 0.9 %copy.3 = f32[160,1536]{1,0:T(8,128)} copy(f32[160,1536]{1,0:T(8,128)S(1)} %shard_map.17) | data formatting | bytes 1966080
